TPU v7x, 32 devices: a whole 2x2x4 slice. The times are simulated.
32 devices in a mesh: shard: 8 (over z, core), batch: 4 (over y, x).
Axes of the slice: x: 2, y: 2, z: 4, core: 2. Of those that a mesh axis runs over, the one named last changes fastest.
Arguments:
- data_inputs: bfloat16 [8, 256, 1024], P('shard', 'batch'), may hold values from -6 to 6
- data_targets: bfloat16 [8, 256, 512], P('shard', 'batch'), may hold values from -6 to 6
- row_picks: int32 [2, 8, 512], P(None, 'shard', 'batch'), may hold values from 0 to 63
- layer_one: float32 [8, 1024, 2048], P('shard', None, 'batch'), may hold values from -6 to 6
- layer_two: float32 [8, 2048, 512], P('shard', 'batch'), may hold values from -6 to 6
- noise_one: bfloat16 [2, 8, 1024, 2048], P(None, 'shard', None, 'batch'), may hold values from -6 to 6
- noise_two: bfloat16 [2, 8, 2048, 512], P(None, 'shard', 'batch'), may hold values from -6 to 6
Outputs:
- moved_one: float32 [8, 1024, 2048], P('shard', None, 'batch')
- moved_two: float32 [8, 2048, 512], P('shard', 'batch')
- last_errors: bfloat16 [8, 512, 512], P('shard', 'batch')
All inputs are finite; a program needn't handle non-finite values.
Results may differ from a plain program's by a relative error of at most 0.014.
Values may be sent and summed in bfloat16 or wider, within the bound.
A program may use at most 64 MiB of HBM per device.

v0:
```python
import jax
import jax.numpy as jnp
from jax import lax
from jax.sharding import PartitionSpec as P

D_IN = 1024
HID = 2048
STEPS = 2
half_step = 0.01
root_step = 0.02**0.5
precision_obs = 32.0


def passed_along(value, axis, by):
    size = lax.axis_size(axis)
    return lax.ppermute(value, axis, [(i, (i + by) % size) for i in range(size)])


def per_device(data_inputs, data_targets, row_picks, layer_one, layer_two, noise_one, noise_two):
    scale_in = D_IN ** (-0.5)
    scale_hid = HID ** (-0.5)
    weights_a = layer_one[0]
    weights_b = layer_two[0]
    contract_rows = (((0,), (0,)), ((), ()))
    contract_cols = (((1,), (1,)), ((), ()))
    own_errors = jnp.zeros((row_picks.shape[2], weights_b.shape[1]), jnp.float32)
    for iteration in range(STEPS):
        chosen = row_picks[iteration, 0]
        local_rows = jnp.take(data_inputs[0], chosen, axis=0)
        local_targets = jnp.take(data_targets[0], chosen, axis=0)
        bf_a = weights_a.astype(jnp.bfloat16)
        bf_b = weights_b.astype(jnp.bfloat16)
        all_rows = lax.all_gather(local_rows, "batch", axis=0, tiled=True)
        hidden = jnp.tanh(jnp.dot(all_rows, bf_a, preferred_element_type=jnp.float32) * scale_in)
        hidden_b = hidden.astype(jnp.bfloat16)
        predicted = lax.psum_scatter(
            (jnp.dot(hidden_b, bf_b, preferred_element_type=jnp.float32) * scale_hid).astype(
                jnp.bfloat16
            ),
            "batch",
            scatter_dimension=0,
            tiled=True,
        ).astype(jnp.float32)
        own_errors = predicted - local_targets.astype(jnp.float32)
        signal = lax.all_gather(
            (precision_obs * own_errors).astype(jnp.bfloat16), "batch", axis=0, tiled=True
        )
        grad_two = (
            lax.dot_general(hidden_b, signal, contract_rows, preferred_element_type=jnp.float32)
            * scale_hid
        )
        back_hidden = (
            lax.dot_general(signal, bf_b, contract_cols, preferred_element_type=jnp.float32)
            * scale_hid
            * (1.0 - hidden * hidden)
        ).astype(jnp.bfloat16)
        grad_one = (
            lax.dot_general(
                all_rows, back_hidden, contract_rows, preferred_element_type=jnp.float32
            )
            * scale_in
        )
        weights_a = (
            weights_a
            - half_step * (grad_one + weights_a)
            + root_step * noise_one[iteration, 0].astype(jnp.float32)
        )
        weights_b = (
            weights_b
            - half_step * (grad_two + weights_b)
            + root_step * noise_two[iteration, 0].astype(jnp.float32)
        )
    moved_a, moved_b = (
        passed_along(weights_a.astype(jnp.bfloat16), "shard", 1).astype(weights_a.dtype),
        passed_along(weights_b.astype(jnp.bfloat16), "shard", 1).astype(weights_b.dtype),
    )
    return (moved_a[None], moved_b[None], own_errors.astype(jnp.bfloat16)[None])


def solution(mesh):
    in_specs = (
        P("shard", "batch", None),
        P("shard", "batch", None),
        P(None, "shard", "batch"),
        P("shard", None, "batch"),
        P("shard", "batch", None),
        P(None, "shard", None, "batch"),
        P(None, "shard", "batch", None),
    )
    out_specs = (P("shard", None, "batch"), P("shard", "batch", None), P("shard", "batch", None))
    return jax.shard_map(
        per_device, mesh=mesh, in_specs=in_specs, out_specs=out_specs, check_vma=False
    )
```

profile of v0, /device:TPU:0, one launch (start us, length us, event | category | flops | bytes accessed | tf_op | source)
XLA Modules:
  0.0 173.4 jit_solution(172406984584624309)
XLA Ops:
  8.1 0.9 gather_fusion
  9.8 30.0 %all-gather.3.cloned.1.call-done = bf16[512,1024]{1,0:T(8,128)(2,1)} async-done(((bf16[128,1024]{1,0:T(8,128)(2,1)}), bf16[512,1024]{1,0:T(8,128)(2,1)}) %all-gather.3.cloned.1.call-update) | async-done | bytes 1048592 | tf_op jit(solution)/shard_map/all_gather | solution.py:33
  39.8 2.6 %fusion.13 = f32[512,512]{1,0:T(8,128)S(1)} fusion(bf16[512,1024]{1,0:T(8,128)(2,1)} %all-gather.3.cloned.1.call-done, f32[1,1024,512]{2,1,0:T(8,128)} %param.14), kind=kOutput, calls=%fused_computation.30 | convolution fusion | flops 537133056 | bytes 4194304 | tf_op jit(solution)/shard_map/dot_general | solution.py:34
  42.4 1.2 fusion.17
  43.8 0.9 gather_fusion.2
  45.5 0.8 gather_fusion.1
  46.4 22.3 %reduce-scatter.3.cloned.1.call-done = bf16[128,512]{1,0:T(8,128)(2,1)} async-done(((bf16[512,512]{1,0:T(8,128)(2,1)}), bf16[128,512]{1,0:T(8,128)(2,1)}) %reduce-scatter.3.cloned.1.call-update) | async-done | bytes 131088 | tf_op jit(solution)/shard_map/reduce_scatter | solution.py:36
  68.6 1.0 multiply_convert_fusion.1
  69.7 10.0 %all_gather.13 = bf16[512,512]{1,0:T(8,128)(2,1)S(1)} all-gather(bf16[128,512]{1,0:T(8,128)(2,1)S(1)} %multiply_convert_fusion.1), channel_id=1, replica_groups=mesh['shard'=8,'batch'=4] {'batch'}, dimensions={0}, use_global_device_ids=true | all-gather | bytes 655360 | tf_op jit(solution)/shard_map/all_gather | solution.py:45
  80.5 1.6 fusion.10
  82.1 5.0 %bitcast_add_fusion.1 = f32[1024,512]{1,0:T(8,128)} fusion(f32[1,1024,512]{2,1,0:T(8,128)} %param.14, bf16[512,1024]{1,0:T(8,128)(2,1)} %all-gather.3.cloned.1.call-done, bf16[512,512]{1,0:T(8,128)(2,1)} %copy-done.3, bf16[2,1,1024,512]{3,2,1,0:T(8,128)(2,1)} %param.16, f32[512,512]{1,0:T(8,128)S(1)} %fusion.13, f32[1,512,512]{2,1,0:T(8,128)S(1)} %copy-done.2), kind=kOutput, calls=%fused_computation.6 | convolution fusion | flops 810287104 | bytes 8912896 | tf_op jit(solution)/shard_map/dot_general | solution.py:58
  87.1 10.2 %all-gather.5.cloned.1.call-done = bf16[512,1024]{1,0:T(8,128)(2,1)} async-done(((bf16[128,1024]{1,0:T(8,128)(2,1)}), bf16[512,1024]{1,0:T(8,128)(2,1)}) %all-gather.5.cloned.1.call-update) | async-done | bytes 1048592 | tf_op jit(solution)/shard_map/all_gather | solution.py:33
  97.3 2.6 %fusion.11 = f32[512,512]{1,0:T(8,128)S(1)} fusion(bf16[512,1024]{1,0:T(8,128)(2,1)} %all-gather.5.cloned.1.call-done, f32[1024,512]{1,0:T(8,128)} %bitcast_add_fusion.1), kind=kOutput, calls=%fused_computation.25 | convolution fusion | flops 537657344 | bytes 4194304 | tf_op jit(solution)/shard_map/dot_general | solution.py:34
  99.9 1.2 fusion.18
  101.2 0.8 gather_fusion.3
  102.1 24.1 %reduce-scatter.5.cloned.1.call-done = bf16[128,512]{1,0:T(8,128)(2,1)} async-done(((bf16[512,512]{1,0:T(8,128)(2,1)}), bf16[128,512]{1,0:T(8,128)(2,1)}) %reduce-scatter.5.cloned.1.call-update) | async-done | bytes 131088 | tf_op jit(solution)/shard_map/reduce_scatter | solution.py:36
  126.2 1.7 fusion.36
  127.8 9.9 %all_gather.15 = bf16[512,512]{1,0:T(8,128)(2,1)S(1)} all-gather(bf16[128,512]{1,0:T(8,128)(2,1)S(1)} %get-tuple-element.10), channel_id=1, replica_groups=mesh['shard'=8,'batch'=4] {'batch'}, dimensions={0}, use_global_device_ids=true | all-gather | bytes 655360 | tf_op jit(solution)/shard_map/all_gather | solution.py:45
  137.8 4.5 %fusion = bf16[1024,512]{1,0:T(8,128)(2,1)} fusion(f32[1024,512]{1,0:T(8,128)} %bitcast_add_fusion.1, bf16[512,1024]{1,0:T(8,128)(2,1)} %all-gather.5.cloned.1.call-done, bf16[512,512]{1,0:T(8,128)(2,1)S(1)} %all_gather.15, bf16[2,1,1024,512]{3,2,1,0:T(8,128)(2,1)} %param.16, f32[512,512]{1,0:T(8,128)S(1)} %fusion.11, f32[512,512]{1,0:T(8,128)S(1)} %fusion.10), kind=kOutput, calls=%fused_computation.5 | convolution fusion | flops 811073536 | bytes 7864320 | tf_op jit(solution)/shard_map/dot_general | solution.py:58
  142.3 1.6 fusion.16
  144.0 1.7 collective-permute-start.1
  145.6 18.6 %collective-permute-done.1 = bf16[512,512]{1,0:T(8,128)(2,1)S(1)} collective-permute-done((bf16[512,512]{1,0:T(8,128)(2,1)S(1)}, bf16[512,512]{1,0:T(8,128)(2,1)S(1)}, u32[]{:S(2)}, u32[]{:S(2)}) %collective-permute-start.1) | collective-permute-done | bytes 524320 | tf_op jit(solution)/shard_map/ppermute | solution.py:16
  164.2 1.1 bitcast_convert_fusion.4
  165.3 1.6 bitcast_convert_fusion.2
  (23 shorter events, 3.5 us)
Async XLA Ops:
  7.2 0.9 copy-start
  7.2 32.6 %all-gather.3.cloned.1.call-start = ((), (), s32[]{:S(2)}) async-start(), calls=%async_computation.2 | async-start | bytes 1310720 | tf_op jit(solution)/shard_map/all_gather | solution.py:33
  9.8 32.7 %copy-start.2 = (f32[1,512,512]{2,1,0:T(8,128)S(1)}, f32[1,512,512]{2,1,0:T(8,128)}, u32[]{:S(2)}) copy-start(f32[1,512,512]{2,1,0:T(8,128)} %param.15) | copy-start | bytes 3145732
  9.8 58.9 %reduce-scatter.3.cloned.1.call-start = ((), (), s32[]{:S(2)}) async-start(), calls=%async_computation.3 | async-start | bytes 655360 | tf_op jit(solution)/shard_map/reduce_scatter | solution.py:36
  43.7 1.8 %copy-start.1 = (bf16[1,64,512]{2,1,0:T(8,128)(2,1)S(1)}, bf16[1,64,512]{2,1,0:T(8,128)(2,1)}, u32[]{:S(2)}) copy-start(bf16[1,64,512]{2,1,0:T(8,128)(2,1)} %param.12) | copy-start | bytes 196612
  43.7 53.6 %all-gather.5.cloned.1.call-start = ((), (), s32[]{:S(2)}) async-start(), calls=%async_computation.4 | async-start | bytes 1310720 | tf_op jit(solution)/shard_map/all_gather | solution.py:33
  45.5 80.7 %reduce-scatter.5.cloned.1.call-start = ((), (), s32[]{:S(2)}) async-start(), calls=%async_computation.5 | async-start | bytes 655360 | tf_op jit(solution)/shard_map/reduce_scatter | solution.py:36
  79.7 0.8 copy-start.3
  142.3 23.0 %collective-permute-start = (bf16[1024,512]{1,0:T(8,128)(2,1)}, bf16[1024,512]{1,0:T(8,128)(2,1)S(1)}, u32[]{:S(2)}, u32[]{:S(2)}) collective-permute-start(bf16[1024,512]{1,0:T(8,128)(2,1)} %fusion), channel_id=1, source_target_pairs={{0,4},{4,8},{8,12},{12,16},{16,20},{20,24},{24,28},{28,0},{1,5},{5... | collective-permute-start | bytes 3145736 | tf_op jit(solution)/shard_map/ppermute | solution.py:16
  144.0 20.2 %collective-permute-start.1 = (bf16[512,512]{1,0:T(8,128)(2,1)S(1)}, bf16[512,512]{1,0:T(8,128)(2,1)S(1)}, u32[]{:S(2)}, u32[]{:S(2)}) collective-permute-start(bf16[512,512]{1,0:T(8,128)(2,1)S(1)} %fusion.16), channel_id=1, source_target_pairs={{0,4},{4,8},{8,12},{12,16},{16,20},{20,24},{24,28},{28,0},{1,5},{5... | collective-permute-start | bytes 1572872 | tf_op jit(solution)/shard_map/ppermute | solution.py:16
Sparse Core Ops, SparseCore 0:
  10.4 29.3 all-gather.2
  43.8 24.7 reduce-scatter.2
  70.6 26.6 all-gather.4
  101.3 24.7 reduce-scatter.4
where the time goes:
time: 174 us; the launch traced here: 173 us
  waiting for transfers between devices  105 us (60%)
  matrix products  20.5 us (12%)
  blocking collectives  20 us (11%)
  between operations  13.8 us (8%)
  other arithmetic  7.74 us (4%)
  local copies, waits for them, and re-layouts  4.36 us (3%)
  starting transfers between devices  1.82 us (1%)
    reduce_scatter x2, waiting for transfers between devices, per_device(): lax.psum_scatter((jnp.dot(hidden_b, bf_b, preferred_element_type=jnp.floa...  46.4 us
    all_gather x2, waiting for transfers between devices, per_device(): all_rows = lax.all_gather(local_rows, 'batch', axis=0, tiled=True)  40.2 us
    all_gather x2, blocking collectives, per_device(): lax.all_gather((precision_obs * own_errors).astype(jnp.bfloat16), 'batch'...  20 us
    ppermute x2, waiting for transfers between devices, passed_along(): lax.ppermute(value, axis, [(i, (i + by) % size) for i in range(size)])  18.6 us
    dot_general x2, matrix products, per_device(): lax.dot_general(all_rows, back_hidden, contract_rows, preferred_element_t...  9.51 us
    dot_general x2, matrix products, per_device(): jnp.dot(all_rows, bf_a, preferred_element_type=jnp.float32) * scale_in  5.27 us
    broadcast_in_dim x3, other arithmetic, per_device(): return (moved_a[None], moved_b[None], own_errors.astype(jnp.bfloat16)[None])  4.4 us
  transfers between devices with their start and end apart: 6, of which 5 were waited for; matrix products, arithmetic and copies ran while one was open for 8% of the time, Pallas kernels for 0%

commit v1 on v0

--- a/solution.py
+++ b/solution.py
@@ -2,6 +2,7 @@
 import jax.numpy as jnp
 from jax import lax
 from jax.sharding import PartitionSpec as P
+from jax.lax import axis_index, axis_size, ppermute
 
 D_IN = 1024
 HID = 2048
@@ -9,6 +10,14 @@
 half_step = 0.01
 root_step = 0.02**0.5
 precision_obs = 32.0
+
+
+def groups_supply_all(message, dim_i):
+    message = jnp.moveaxis(message, 0, dim_i)
+    part_next = message.shape
+    return message.reshape(
+        *part_next[:dim_i], part_next[dim_i] * part_next[dim_i + 1], *part_next[dim_i + 2 :]
+    )
 
 
 def passed_along(value, axis, by):
@@ -30,7 +39,23 @@
         local_targets = jnp.take(data_targets[0], chosen, axis=0)
         bf_a = weights_a.astype(jnp.bfloat16)
         bf_b = weights_b.astype(jnp.bfloat16)
-        all_rows = lax.all_gather(local_rows, "batch", axis=0, tiled=True)
+        nodes = axis_size("batch")
+        frames = [(it, (it + 1) % nodes) for it in range(nodes)]
+        all_blocks = [(kk, hop_no) for hop_no, kk in frames]
+        taken_in, view_out = ([], [])
+        for c in range(nodes - 1):
+            if c % 2 == 0:
+                outer = ppermute(taken_in[-1] if taken_in else local_rows, "batch", frames)
+                taken_in.append(outer)
+            else:
+                upper = ppermute(view_out[-1] if view_out else local_rows, "batch", all_blocks)
+                view_out.append(upper)
+        field_out = jnp.stack([*taken_in[::-1], local_rows, *view_out], axis=0)
+        b_next = axis_index("batch")
+        carry_in = len(taken_in)
+        block_out = b_next - carry_in
+        field_out = field_out[(jnp.arange(nodes) - block_out) % nodes]
+        all_rows = groups_supply_all(field_out, 0)
         hidden = jnp.tanh(jnp.dot(all_rows, bf_a, preferred_element_type=jnp.float32) * scale_in)
         hidden_b = hidden.astype(jnp.bfloat16)
         predicted = lax.psum_scatter(

time: 174 us -> 161 us (0.925)
  waiting for transfers between devices: 105 us -> 78.1 us
  starting transfers between devices: 1.82 us -> 9.78 us
  other arithmetic: 7.74 us -> 11.5 us
  local copies, waits for them, and re-layouts: 4.36 us -> 7.94 us
  matrix products: 20.5 us -> 18.3 us
    all_gather x2 -> x0, waiting for transfers between devices: 40.2 us -> none  [per_device(): all_rows = lax.all_gather(local_rows, 'batch', axis=0, tiled=True)]
    ppermute x0 -> x6, waiting for transfers between devices: none -> 35.3 us  [the longest x4 26.3 us: per_device(): outer = ppermute(taken_in[-1] if taken_in else local_rows, 'batch', frames)]
    reduce_scatter x2, waiting for transfers between devices: 46.4 us -> 24.4 us  [per_device(): lax.psum_scatter((jnp.dot(hidden_b, bf_b, preferred_element_type=jnp.floa...]
    ppermute x0 -> x6, starting transfers between devices: none -> 8.04 us  [the longest x4 4.88 us: per_device(): outer = ppermute(taken_in[-1] if taken_in else local_rows, 'batch', frames)]
    another operation x0 -> x4, other arithmetic: none -> 3.48 us  [per_device(): field_out = jnp.stack([*taken_in[::-1], local_rows, *view_out], axis=0)]
    gather x0 -> x2, local copies, waits for them, and re-layouts: none -> 3.42 us  [per_device(): field_out = field_out[(jnp.arange(nodes) - block_out) % nodes]]
    dot_general x2, matrix products: 5.27 us -> 3.11 us  [per_device(): jnp.dot(all_rows, bf_a, preferred_element_type=jnp.float32) * scale_in]
  transfers between devices with their start and end apart: 6 -> 10, of which waited for: 5 -> 8; matrix products, arithmetic and copies ran while one was open for 8% -> 9% of each run, Pallas kernels for 0% -> 0%
where the time goes in v1:
time: 161 us
  waiting for transfers between devices  78.1 us (49%)
  blocking collectives  21.5 us (13%)
  matrix products  18.3 us (11%)
  between operations  14.2 us (9%)
  other arithmetic  11.5 us (7%)
  starting transfers between devices  9.78 us (6%)
  local copies, waits for them, and re-layouts  7.94 us (5%)
    ppermute x4, waiting for transfers between devices, per_device(): outer = ppermute(taken_in[-1] if taken_in else local_rows, 'batch', frames)  26.3 us
    reduce_scatter x2, waiting for transfers between devices, per_device(): lax.psum_scatter((jnp.dot(hidden_b, bf_b, preferred_element_type=jnp.floa...  24.4 us
    all_gather x2, blocking collectives, per_device(): lax.all_gather((precision_obs * own_errors).astype(jnp.bfloat16), 'batch'...  21.5 us
    ppermute x2, waiting for transfers between devices, passed_along(): lax.ppermute(value, axis, [(i, (i + by) % size) for i in range(size)])  18.4 us
    dot_general x2, matrix products, per_device(): lax.dot_general(all_rows, back_hidden, contract_rows, preferred_element_t...  8.98 us
    ppermute x2, waiting for transfers between devices, per_device(): ppermute(view_out[-1] if view_out else local_rows, 'batch', all_blocks)  8.94 us
    ppermute x4, starting transfers between devices, per_device(): outer = ppermute(taken_in[-1] if taken_in else local_rows, 'batch', frames)  4.88 us
    broadcast_in_dim x3, other arithmetic, per_device(): return (moved_a[None], moved_b[None], own_errors.astype(jnp.bfloat16)[None])  4.4 us
  transfers between devices with their start and end apart: 10, of which 8 were waited for; matrix products, arithmetic and copies ran while one was open for 9% of the time, Pallas kernels for 0%

profile of v1, /device:TPU:0, one launch (start us, length us, event | category | flops | bytes accessed | tf_op | source)
XLA Modules:
  0.0 161.1 jit_solution(6257982826045063101)
XLA Ops:
  9.0 3.0 %collective-permute-start = (bf16[128,1024]{1,0:T(8,128)(2,1)S(1)}, bf16[128,1024]{1,0:T(8,128)(2,1)S(1)}, u32[]{:S(2)}, u32[]{:S(2)}) collective-permute-start(bf16[128,1024]{1,0:T(8,128)(2,1)S(1)} %broadcast_select_fusion.1), channel_id=1, source_target_pairs={{0,1},{1,2},{2,3},{3,0},{4,5},{5,6},{6,7},{7,4},{8,9},{9,10},{10,1... | collective-permute-start | bytes 786440 | tf_op jit(solution)/shard_map/ppermute | solution.py:48
  13.1 7.1 %collective-permute-done = bf16[128,1024]{1,0:T(8,128)(2,1)S(1)} collective-permute-done((bf16[128,1024]{1,0:T(8,128)(2,1)S(1)}, bf16[128,1024]{1,0:T(8,128)(2,1)S(1)}, u32[]{:S(2)}, u32[]{:S(2)}) %collective-permute-start) | collective-permute-done | bytes 262176 | tf_op jit(solution)/shard_map/ppermute | solution.py:48
  21.3 5.0 %collective-permute-done.2 = bf16[128,1024]{1,0:T(8,128)(2,1)S(1)} collective-permute-done((bf16[128,1024]{1,0:T(8,128)(2,1)S(1)}, bf16[128,1024]{1,0:T(8,128)(2,1)S(1)}, u32[]{:S(2)}, u32[]{:S(2)}) %collective-permute-start.2) | collective-permute-done | bytes 262176 | tf_op jit(solution)/shard_map/ppermute | solution.py:51
  26.3 4.2 %collective-permute-done.1 = bf16[128,1024]{1,0:T(8,128)(2,1)S(1)} collective-permute-done((bf16[128,1024]{1,0:T(8,128)(2,1)S(1)}, bf16[128,1024]{1,0:T(8,128)(2,1)S(1)}, u32[]{:S(2)}, u32[]{:S(2)}) %collective-permute-start.1) | collective-permute-done | bytes 262176 | tf_op jit(solution)/shard_map/ppermute | solution.py:48
  31.3 2.4 %fusion.13 = f32[512,512]{1,0:T(8,128)S(1)} fusion(bf16[512,1024]{1,0:T(8,128)(2,1)S(1)} %bitcast.79, f32[1,1024,512]{2,1,0:T(8,128)} %param.14), kind=kOutput, calls=%fused_computation.31 | convolution fusion | flops 537657344 | bytes 4194304 | tf_op jit(solution)/shard_map/dot_general | solution.py:59
  35.0 1.6 gather_fusion.4
  36.6 1.7 %broadcast_select_fusion = bf16[128,1024]{1,0:T(8,128)(2,1)} fusion(bf16[128,1024]{1,0:T(8,128)(2,1)} %gather_fusion.4, pred[128]{0:T(512)(128)(4,1)S(1)} %get-tuple-element.5), kind=kLoop, calls=%fused_computation.62 | loop fusion | flops 131072 | bytes 524416 | tf_op jit(solution)/shard_map/jit(_take)/select_n | solution.py:38
  39.1 2.1 %collective-permute-start.5 = (bf16[128,1024]{1,0:T(8,128)(2,1)}, bf16[128,1024]{1,0:T(8,128)(2,1)}, u32[]{:S(2)}, u32[]{:S(2)}) collective-permute-start(bf16[128,1024]{1,0:T(8,128)(2,1)} %broadcast_select_fusion), channel_id=1, source_target_pairs={{1,0},{2,1},{3,2},{0,3},{5,4},{6,5},{7,6},{4,7},{9,8},{10,9},{11,1... | collective-permute-start | bytes 786440 | tf_op jit(solution)/shard_map/ppermute | solution.py:51
  41.3 10.3 %collective-permute-done.3 = bf16[128,1024]{1,0:T(8,128)(2,1)} collective-permute-done((bf16[128,1024]{1,0:T(8,128)(2,1)}, bf16[128,1024]{1,0:T(8,128)(2,1)}, u32[]{:S(2)}, u32[]{:S(2)}) %collective-permute-start.3) | collective-permute-done | bytes 262176 | tf_op jit(solution)/shard_map/ppermute | solution.py:48
  53.5 4.0 %collective-permute-done.5 = bf16[128,1024]{1,0:T(8,128)(2,1)} collective-permute-done((bf16[128,1024]{1,0:T(8,128)(2,1)}, bf16[128,1024]{1,0:T(8,128)(2,1)}, u32[]{:S(2)}, u32[]{:S(2)}) %collective-permute-start.5) | collective-permute-done | bytes 262176 | tf_op jit(solution)/shard_map/ppermute | solution.py:51
  57.5 4.7 %collective-permute-done.4 = bf16[128,1024]{1,0:T(8,128)(2,1)} collective-permute-done((bf16[128,1024]{1,0:T(8,128)(2,1)}, bf16[128,1024]{1,0:T(8,128)(2,1)}, u32[]{:S(2)}, u32[]{:S(2)}) %collective-permute-start.4) | collective-permute-done | bytes 262176 | tf_op jit(solution)/shard_map/ppermute | solution.py:48
  62.2 2.2 %pad_maximum_fusion.1 = bf16[4,128,1024]{2,1,0:T(8,128)(2,1)} fusion(bf16[1,128,1024]{2,1,0:T(8,128)(2,1)} %bitcast.17, bf16[1,128,1024]{2,1,0:T(8,128)(2,1)S(1)} %fusion.60, bf16[1,128,1024]{2,1,0:T(8,128)(2,1)} %bitcast.15, bf16[1,128,1024]{2,1,0:T(8,128)(2,1)} %bitcast.14), kind=kLoop, calls=%fused_computation.38 | loop fusion | flops 1572864 | bytes 2097152 | tf_op jit(solution)/shard_map/stack | solution.py:53
  64.4 2.8 %gather_fusion.1 = bf16[4,128,1024]{2,1,0:T(8,128)(2,1)} fusion(bf16[4,128,1024]{2,1,0:T(8,128)(2,1)} %pad_maximum_fusion.1, s32[1024]{0:T(1024)S(1)} %pad_clamp_fusion.1), kind=kCustom, calls=%fused_computation.5 | custom fusion | bytes 2097168 | tf_op jit(solution)/shard_map/gather | solution.py:57
  68.2 10.9 %all_gather.6 = bf16[512,512]{1,0:T(8,128)(2,1)} all-gather(bf16[128,512]{1,0:T(8,128)(2,1)S(1)} %multiply_convert_fusion.1), channel_id=1, replica_groups=mesh['shard'=8,'batch'=4] {'batch'}, dimensions={0}, use_global_device_ids=true | all-gather | bytes 655360 | tf_op jit(solution)/shard_map/all_gather | solution.py:70
  79.1 4.6 %bitcast_add_fusion.1 = f32[1024,512]{1,0:T(8,128)} fusion(f32[1,1024,512]{2,1,0:T(8,128)} %param.14, bf16[512,1024]{1,0:T(8,128)(2,1)S(1)} %bitcast.80, bf16[512,512]{1,0:T(8,128)(2,1)} %all_gather.6, bf16[2,1,1024,512]{3,2,1,0:T(8,128)(2,1)} %param.16, f32[512,512]{1,0:T(8,128)S(1)} %fusion.13, f32[1,512,512]{2,1,0:T(8,128)S(1)} %copy-done.2), kind=kOutput, calls=%fused_computation.8 | convolution fusion | flops 810287104 | bytes 8912896 | tf_op jit(solution)/shard_map/dot_general | solution.py:83
  83.7 1.9 %fusion.10 = f32[512,512]{1,0:T(8,128)S(1)} fusion(bf16[512,512]{1,0:T(8,128)(2,1)} %all_gather.6, f32[1,512,512]{2,1,0:T(8,128)S(1)} %copy-done.2, bf16[2,1,512,512]{3,2,1,0:T(8,128)(2,1)} %param.17, f32[512,512]{1,0:T(8,128)S(1)} %fusion.13), kind=kOutput, calls=%fused_computation.24 | convolution fusion | flops 270532608 | bytes 4194304 | tf_op jit(solution)/shard_map/dot_general | solution.py:74
  88.8 24.4 %reduce-scatter.5.cloned.1.call-done = bf16[128,512]{1,0:T(8,128)(2,1)} async-done(((bf16[512,512]{1,0:T(8,128)(2,1)}), bf16[128,512]{1,0:T(8,128)(2,1)}) %reduce-scatter.5.cloned.1.call-update) | async-done | bytes 131088 | tf_op jit(solution)/shard_map/reduce_scatter | solution.py:61
  113.1 1.7 %fusion.38 = (bf16[1,128,512]{2,1,0:T(8,128)(2,1)}, bf16[128,512]{1,0:T(8,128)(2,1)S(1)}) fusion(bf16[128,512]{1,0:T(8,128)(2,1)} %reduce-scatter.5.cloned.1.call-done, bf16[128,512]{1,0:T(8,128)(2,1)S(1)} %gather_fusion.5, pred[128]{0:T(512)(128)(4,1)S(1)} %get-tuple-element.5), kind=kLoop, calls=%fused_computation.65 | loop fusion | flops 458752 | bytes 524416 | tf_op jit(solution)/shard_map/broadcast_in_dim | solution.py:102
  114.8 10.6 %all_gather.7 = bf16[512,512]{1,0:T(8,128)(2,1)} all-gather(bf16[128,512]{1,0:T(8,128)(2,1)S(1)} %get-tuple-element.10), channel_id=1, replica_groups=mesh['shard'=8,'batch'=4] {'batch'}, dimensions={0}, use_global_device_ids=true | all-gather | bytes 655360 | tf_op jit(solution)/shard_map/all_gather | solution.py:70
  125.4 4.3 %fusion = bf16[1024,512]{1,0:T(8,128)(2,1)} fusion(f32[1024,512]{1,0:T(8,128)} %bitcast_add_fusion.1, bf16[512,1024]{1,0:T(8,128)(2,1)S(1)} %bitcast.82, bf16[512,512]{1,0:T(8,128)(2,1)} %all_gather.7, bf16[2,1,1024,512]{3,2,1,0:T(8,128)(2,1)} %param.16, f32[512,512]{1,0:T(8,128)S(1)} %fusion.11, f32[512,512]{1,0:T(8,128)S(1)} %fusion.10), kind=kOutput, calls=%fused_computation.7 | convolution fusion | flops 811073536 | bytes 7864320 | tf_op jit(solution)/shard_map/dot_general | solution.py:83
  129.7 1.8 %fusion.16 = bf16[512,512]{1,0:T(8,128)(2,1)S(1)} fusion(f32[512,512]{1,0:T(8,128)S(1)} %fusion.10, bf16[512,512]{1,0:T(8,128)(2,1)} %all_gather.7, bf16[2,1,512,512]{3,2,1,0:T(8,128)(2,1)} %param.17, f32[512,512]{1,0:T(8,128)S(1)} %fusion.11), kind=kOutput, calls=%fused_computation.34 | convolution fusion | flops 270794752 | bytes 3670016 | tf_op jit(solution)/shard_map/dot_general | solution.py:74
  131.5 1.7 %collective-permute-start.7 = (bf16[512,512]{1,0:T(8,128)(2,1)S(1)}, bf16[512,512]{1,0:T(8,128)(2,1)S(1)}, u32[]{:S(2)}, u32[]{:S(2)}) collective-permute-start(bf16[512,512]{1,0:T(8,128)(2,1)S(1)} %fusion.16), channel_id=1, source_target_pairs={{0,4},{4,8},{8,12},{12,16},{16,20},{20,24},{24,28},{28,0},{1,5},{5... | collective-permute-start | bytes 1572872 | tf_op jit(solution)/shard_map/ppermute | solution.py:25
  133.2 18.4 %collective-permute-done.7 = bf16[512,512]{1,0:T(8,128)(2,1)S(1)} collective-permute-done((bf16[512,512]{1,0:T(8,128)(2,1)S(1)}, bf16[512,512]{1,0:T(8,128)(2,1)S(1)}, u32[]{:S(2)}, u32[]{:S(2)}) %collective-permute-start.7) | collective-permute-done | bytes 524320 | tf_op jit(solution)/shard_map/ppermute | solution.py:25
  152.7 1.6 %bitcast_convert_fusion = f32[1,1024,512]{2,1,0:T(8,128)} fusion(bf16[1024,512]{1,0:T(8,128)(2,1)S(1)} %collective-permute-done.6), kind=kLoop, calls=%fused_computation.39 | loop fusion | flops 524288 | bytes 3145728 | tf_op jit(solution)/shard_map/broadcast_in_dim | solution.py:102
  (41 shorter events, 14.0 us)
Async XLA Ops:
  7.2 0.9 copy-start
  7.2 60.0 %reduce-scatter.3.cloned.1.call-start = ((), (), s32[]{:S(2)}) async-start(), calls=%async_computation.2 | async-start | bytes 655360 | tf_op jit(solution)/shard_map/reduce_scatter | solution.py:61
  9.0 11.1 %collective-permute-start = (bf16[128,1024]{1,0:T(8,128)(2,1)S(1)}, bf16[128,1024]{1,0:T(8,128)(2,1)S(1)}, u32[]{:S(2)}, u32[]{:S(2)}) collective-permute-start(bf16[128,1024]{1,0:T(8,128)(2,1)S(1)} %broadcast_select_fusion.1), channel_id=1, source_target_pairs={{0,1},{1,2},{2,3},{3,0},{4,5},{5,6},{6,7},{7,4},{8,9},{9,10},{10,1... | collective-permute-start | bytes 786440 | tf_op jit(solution)/shard_map/ppermute | solution.py:48
  12.0 14.3 %collective-permute-start.2 = (bf16[128,1024]{1,0:T(8,128)(2,1)S(1)}, bf16[128,1024]{1,0:T(8,128)(2,1)S(1)}, u32[]{:S(2)}, u32[]{:S(2)}) collective-permute-start(bf16[128,1024]{1,0:T(8,128)(2,1)S(1)} %broadcast_select_fusion.1), channel_id=1, source_target_pairs={{1,0},{2,1},{3,2},{0,3},{5,4},{6,5},{7,6},{4,7},{9,8},{10,9},{11,1... | collective-permute-start | bytes 786440 | tf_op jit(solution)/shard_map/ppermute | solution.py:51
  20.1 10.4 %collective-permute-start.1 = (bf16[128,1024]{1,0:T(8,128)(2,1)S(1)}, bf16[128,1024]{1,0:T(8,128)(2,1)S(1)}, u32[]{:S(2)}, u32[]{:S(2)}) collective-permute-start(bf16[128,1024]{1,0:T(8,128)(2,1)S(1)} %collective-permute-done), channel_id=1, source_target_pairs={{0,1},{1,2},{2,3},{3,0},{4,5},{5,6},{6,7},{7,4},{8,9},{9,10},{10,1... | collective-permute-start | bytes 786440 | tf_op jit(solution)/shard_map/ppermute | solution.py:48
  31.3 2.4 %copy-start.2 = (f32[1,512,512]{2,1,0:T(8,128)S(1)}, f32[1,512,512]{2,1,0:T(8,128)}, u32[]{:S(2)}) copy-start(f32[1,512,512]{2,1,0:T(8,128)} %param.15) | copy-start | bytes 3145732
  34.9 16.7 %copy-start.1 = (bf16[1,64,512]{2,1,0:T(8,128)(2,1)S(1)}, bf16[1,64,512]{2,1,0:T(8,128)(2,1)}, u32[]{:S(2)}) copy-start(bf16[1,64,512]{2,1,0:T(8,128)(2,1)} %param.12) | copy-start | bytes 196612
  35.0 78.1 %reduce-scatter.5.cloned.1.call-start = ((), (), s32[]{:S(2)}) async-start(), calls=%async_computation.3 | async-start | bytes 655360 | tf_op jit(solution)/shard_map/reduce_scatter | solution.py:61
  38.3 13.3 %collective-permute-start.3 = (bf16[128,1024]{1,0:T(8,128)(2,1)}, bf16[128,1024]{1,0:T(8,128)(2,1)}, u32[]{:S(2)}, u32[]{:S(2)}) collective-permute-start(bf16[128,1024]{1,0:T(8,128)(2,1)} %broadcast_select_fusion), channel_id=1, source_target_pairs={{0,1},{1,2},{2,3},{3,0},{4,5},{5,6},{6,7},{7,4},{8,9},{9,10},{10,1... | collective-permute-start | bytes 786440 | tf_op jit(solution)/shard_map/ppermute | solution.py:48
  39.1 18.3 %collective-permute-start.5 = (bf16[128,1024]{1,0:T(8,128)(2,1)}, bf16[128,1024]{1,0:T(8,128)(2,1)}, u32[]{:S(2)}, u32[]{:S(2)}) collective-permute-start(bf16[128,1024]{1,0:T(8,128)(2,1)} %broadcast_select_fusion), channel_id=1, source_target_pairs={{1,0},{2,1},{3,2},{0,3},{5,4},{6,5},{7,6},{4,7},{9,8},{10,9},{11,1... | collective-permute-start | bytes 786440 | tf_op jit(solution)/shard_map/ppermute | solution.py:51
  51.6 10.6 %collective-permute-start.4 = (bf16[128,1024]{1,0:T(8,128)(2,1)}, bf16[128,1024]{1,0:T(8,128)(2,1)}, u32[]{:S(2)}, u32[]{:S(2)}) collective-permute-start(bf16[128,1024]{1,0:T(8,128)(2,1)} %collective-permute-done.3), channel_id=1, source_target_pairs={{0,1},{1,2},{2,3},{3,0},{4,5},{5,6},{6,7},{7,4},{8,9},{9,10},{10,1... | collective-permute-start | bytes 786440 | tf_op jit(solution)/shard_map/ppermute | solution.py:48
  83.7 1.9 %copy-start.3 = (f32[1024,512]{1,0:T(8,128)S(1)}, f32[1024,512]{1,0:T(8,128)}, u32[]{:S(2)}) copy-start(f32[1024,512]{1,0:T(8,128)} %bitcast_add_fusion.1) | copy-start | bytes 6291460
  83.7 2.2 %copy-start.4 = (bf16[4,128,1024]{2,1,0:T(8,128)(2,1)S(1)}, bf16[4,128,1024]{2,1,0:T(8,128)(2,1)}, u32[]{:S(2)}) copy-start(bf16[4,128,1024]{2,1,0:T(8,128)(2,1)} %gather_fusion.1) | copy-start | bytes 3145732
  87.9 37.5 %copy-start.5 = (bf16[4,128,1024]{2,1,0:T(8,128)(2,1)S(1)}, bf16[4,128,1024]{2,1,0:T(8,128)(2,1)}, u32[]{:S(2)}) copy-start(bf16[4,128,1024]{2,1,0:T(8,128)(2,1)} %gather_fusion.1) | copy-start | bytes 3145732
  129.7 23.0 %collective-permute-start.6 = (bf16[1024,512]{1,0:T(8,128)(2,1)}, bf16[1024,512]{1,0:T(8,128)(2,1)S(1)}, u32[]{:S(2)}, u32[]{:S(2)}) collective-permute-start(bf16[1024,512]{1,0:T(8,128)(2,1)} %fusion), channel_id=1, source_target_pairs={{0,4},{4,8},{8,12},{12,16},{16,20},{20,24},{24,28},{28,0},{1,5},{5... | collective-permute-start | bytes 3145736 | tf_op jit(solution)/shard_map/ppermute | solution.py:25
  131.5 20.1 %collective-permute-start.7 = (bf16[512,512]{1,0:T(8,128)(2,1)S(1)}, bf16[512,512]{1,0:T(8,128)(2,1)S(1)}, u32[]{:S(2)}, u32[]{:S(2)}) collective-permute-start(bf16[512,512]{1,0:T(8,128)(2,1)S(1)} %fusion.16), channel_id=1, source_target_pairs={{0,4},{4,8},{8,12},{12,16},{16,20},{20,24},{24,28},{28,0},{1,5},{5... | collective-permute-start | bytes 1572872 | tf_op jit(solution)/shard_map/ppermute | solution.py:25
Sparse Core Ops, SparseCore 0:
  35.1 28.2 reduce-scatter.2
  88.0 25.0 reduce-scatter.4
